TPU v7x, 128 devices: a whole 4x4x4 slice. The times are simulated.
128 devices in a mesh: row: 8 (over z, x_hi), col: 16 (over x_lo, y, core).
Axes of the slice: x: 4 (x_hi: 2, x_lo: 2; x = x_hi * 2 + x_lo), y: 4, z: 4, core: 2. Of those that a mesh axis runs over, the one named last changes fastest.
Arguments:
- pair: bfloat16 [1024, 1024, 128], P(('row', 'col')), may hold values from -6 to 6
- residue_mask: int32 [1024], replicated, may hold values from 0 to 1, as said below
- ln_gain: float32 [2, 128], replicated, may hold values from 0.5 to 1.5
- ln_shift: float32 [2, 128], replicated, may hold values from -3 to 3
- w_proj: bfloat16 [2, 128, 512], replicated, may hold values from -0.5 to 0.5
- w_bias: bfloat16 [2, 128, 4], replicated, may hold values from -10.606602 to 10.606602
- gate_bias: float32 [2, 128], replicated, may hold values from -4 to 4
- w_out: bfloat16 [2, 128, 128], replicated, may hold values from -0.5 to 0.5
- out_bias: float32 [2, 128], replicated, may hold values from -3 to 3
Outputs:
- starting_update: bfloat16 [256, 1024, 128], P(('row', 'col'))
- ending_update: bfloat16 [256, 1024, 128], P(('row', 'col'))
Inputs may be any that keep to these rules, and one draw needn't show every extreme that they name: `residue_mask`: residue 0 is always a real residue.
All inputs are finite; a program needn't handle non-finite values.
Results may differ from a plain program's by a relative error of at most 0.0065.
The roundings to bfloat16 on the way count: a program that leaves them out, or rounds other values in their place, can miss the bound.
Values may be sent and summed in bfloat16 or wider, within the bound.
A program may use at most 128 MiB of HBM per device.

v0:
```python
import jax
import jax.numpy as jnp
from jax import lax
from jax.sharding import PartitionSpec as P

WD = 2


EPS = 1e-05


def layer_norm(values, gain, shift):
    wide = values.astype(jnp.float32)
    center = jnp.mean(wide, -1, keepdims=True)
    spread = jnp.mean(jnp.square(wide - center), -1, keepdims=True)
    return ((wide - center) * lax.rsqrt(spread + EPS) * gain + shift).astype(jnp.bfloat16)


def project(normed, weight, offset, head_count):
    lead = normed.shape[:-1]
    inner = weight.shape[1] // 4
    size = inner // head_count
    full = jnp.dot(normed.reshape(-1, normed.shape[-1]), weight, preferred_element_type=jnp.float32)
    queries = (
        (full[:, :inner] * size ** (-0.5)).astype(jnp.bfloat16).reshape(lead + (head_count, size))
    )
    key_rows = full[:, inner : 2 * inner].astype(jnp.bfloat16).reshape(lead + (head_count, size))
    value_rows = (
        full[:, 2 * inner : 3 * inner].astype(jnp.bfloat16).reshape(lead + (head_count, size))
    )
    gating = jax.nn.sigmoid(full[:, 3 * inner :] + offset).reshape(lead + (inner,))
    return (queries, key_rows, value_rows, gating)


def attend(queries, key_rows, value_rows, gating, bias, live, weight_out, offset_out):
    scores = jnp.einsum(
        "qhd,khd->hqk", queries, key_rows, preferred_element_type=jnp.float32
    ) + bias.astype(jnp.float32)
    scores = jnp.where(live[None, None, :] > 0, scores, jnp.float32(-1000000000.0))
    top = jnp.max(scores, -1, keepdims=True)
    expo = jnp.exp(scores - top)
    weights = (expo / jnp.sum(expo, -1, keepdims=True)).astype(jnp.bfloat16)
    mixed = jnp.einsum("hqk,khd->qhd", weights, value_rows, preferred_element_type=jnp.float32)
    gated = (mixed.reshape(mixed.shape[0], -1) * gating).astype(jnp.bfloat16)
    return (jnp.dot(gated, weight_out, preferred_element_type=jnp.float32) + offset_out).astype(
        jnp.bfloat16
    )


def attend_lines(queries, key_rows, value_rows, gating, bias, live, weight_out, offset_out):
    lines, count = (queries.shape[0], queries.shape[1])
    scores = (
        jnp.einsum("wqhd,wkhd->whqk", queries, key_rows, preferred_element_type=jnp.float32)
        + bias.astype(jnp.float32)[None]
    )
    scores = jnp.where(live[None, None, None, :] > 0, scores, jnp.float32(-1000000000.0))
    top = jnp.max(scores, -1, keepdims=True)
    expo = jnp.exp(scores - top)
    weights = (expo / jnp.sum(expo, -1, keepdims=True)).astype(jnp.bfloat16)
    mixed = jnp.einsum("whqk,wkhd->wqhd", weights, value_rows, preferred_element_type=jnp.float32)
    gated = (mixed.reshape(lines, count, -1) * gating).astype(jnp.bfloat16)
    flat = (
        jnp.dot(gated.reshape(lines * count, -1), weight_out, preferred_element_type=jnp.float32)
        + offset_out
    )
    return flat.astype(jnp.bfloat16).reshape(lines, count, -1)


def local_bias(normed, weight):
    rows, length, channels = normed.shape
    flat = jnp.dot(normed.reshape(-1, channels), weight, preferred_element_type=jnp.float32)
    return jnp.transpose(flat.astype(jnp.bfloat16).reshape(rows, length, -1), (2, 0, 1))


def body(pair, residue_mask, ln_gain, ln_shift, w_proj, w_bias, gate_bias, w_out, out_bias):
    rows, length, channels = pair.shape
    head_count = w_bias.shape[2]
    devices = lax.axis_size("row") * lax.axis_size("col")
    width = WD
    normed_start = layer_norm(pair, ln_gain[0], ln_shift[0])
    normed_end = layer_norm(pair, ln_gain[1], ln_shift[1])
    bias_start = local_bias(normed_start, w_bias[0])
    bias_end = local_bias(normed_end, w_bias[1])
    start_q, start_k, start_v, start_g = project(
        normed_start[:width], w_proj[0], gate_bias[0], head_count
    )
    starting_update = attend_lines(
        start_q,
        start_k,
        start_v,
        start_g,
        lax.all_gather(bias_start, ("row", "col"), axis=1, tiled=True),
        residue_mask,
        w_out[0],
        out_bias[0],
    )
    end_full = None
    picked = pair.reshape(rows, devices, rows, channels)[:, :, :width, :]
    moved = lax.all_to_all(picked, ("row", "col"), split_axis=1, concat_axis=1, tiled=True)
    columns = jnp.transpose(moved, (2, 1, 0, 3)).reshape(width, length, channels)
    end_full = lax.all_gather(bias_end, ("row", "col"), axis=1, tiled=True)
    end_table = jnp.transpose(end_full, (0, 2, 1))
    normed_columns = layer_norm(columns, ln_gain[1], ln_shift[1])
    end_q, end_k, end_v, end_g = project(normed_columns, w_proj[1], gate_bias[1], head_count)

    def end_line(item):
        queries, key_rows, value_rows, gating = item
        return attend(
            queries, key_rows, value_rows, gating, end_table, residue_mask, w_out[1], out_bias[1]
        )

    ending_update = lax.map(end_line, (end_q, end_k, end_v, end_g))
    return (starting_update, ending_update)


def solution(mesh):
    return jax.shard_map(
        body,
        mesh=mesh,
        in_specs=(P(("row", "col"), None, None), P(), P(), P(), P(), P(), P(), P(), P()),
        out_specs=(P(("row", "col"), None, None), P(("row", "col"), None, None)),
        check_vma=False,
    )
```

profile of v0, /device:TPU:1, one launch (start us, length us, event | category | flops | bytes accessed | tf_op | source)
XLA Modules:
  0.0 239.6 jit_solution(6539840758514527280)
XLA Ops:
  7.2 2.2 convert_reduce_fusion
  9.5 3.6 %fusion.52 = f32[8,1024]{1,0:T(8,128)S(1)} fusion(bf16[8,1024,128]{2,1,0:T(8,128)(2,1)} %param.11, f32[8,1024]{1,0:T(8,128)S(1)} %broadcast_multiply_fusion.1), kind=kLoop, calls=%fused_computation.60 | loop fusion | flops 4186112 | bytes 2162688 | tf_op jit(solution)/shard_map/reduce_sum | solution.py:15
  13.9 4.9 %fusion.51 = (bf16[8,1024,128]{2,1,0:T(8,128)(2,1)S(1)}, bf16[8,1024,128]{2,1,0:T(8,128)(2,1)S(1)}) fusion(bf16[8,1024,128]{2,1,0:T(8,128)(2,1)} %param.11, f32[128]{0:T(128)S(1)} %get-tuple-element.137, f32[128]{0:T(128)S(1)} %get-tuple-element.146, f32[8,1024]{1,0:T(8,128)S(1)} %add_rsqrt_fusion.1, f32[8,1024]{1,0:T(8,128)S(1)} %broadcast_multiply_fusion.1, ...), kind=kLoop, calls=%fused_computation.59 | loop fusion | flops 9437184 | bytes 6359040 | tf_op jit(solution)/shard_map/convert_element_type | solution.py:16
  20.2 1.3 convolution_convert_fusion.1
  21.5 1.9 slice.105
  24.5 11.5 %all-to-all-start = ((bf16[8,128,2,128]{3,2,0,1:T(2,128)(2,1)}), bf16[8,128,2,128]{3,2,0,1:T(2,128)(2,1)S(1)}, u32[]{:S(2)}, u32[]{:S(2)}) async-start(bf16[8,128,2,128]{3,2,0,1:T(2,128)(2,1)} %copy.93), calls=%async_computation | async-start | bytes 1048576 | tf_op jit(solution)/shard_map/all_to_all | solution.py:99
  36.9 2.0 copy-done
  44.4 5.6 %all-to-all-done = bf16[8,128,2,128]{3,2,0,1:T(2,128)(2,1)S(1)} async-done(((bf16[8,128,2,128]{3,2,0,1:T(2,128)(2,1)}), bf16[8,128,2,128]{3,2,0,1:T(2,128)(2,1)S(1)}, u32[]{:S(2)}, u32[]{:S(2)}) %all-to-all-start) | async-done | bytes 524320 | tf_op jit(solution)/shard_map/all_to_all | solution.py:99
  51.8 2.6 %fusion.119 = (bf16[2048,512]{1,0:T(8,128)(2,1)S(1)}, f32[2048,512]{1,0:T(8,128)}) fusion(bf16[2048,128]{1,0:T(8,128)(2,1)S(1)} %bitcast.160, bf16[2,128,512]{2,1,0:T(8,128)(2,1)S(1)} %copy-done.5), kind=kOutput, calls=%fused_computation.127 | convolution fusion | flops 269484032 | bytes 6946816 | tf_op jit(solution)/shard_map/dot_general | solution.py:23
  56.7 1.8 fusion.60
  59.3 36.1 %all-gather.5.cloned.1.call-done = bf16[4,1024,1024]{2,1,0:T(8,128)(2,1)} async-done(((bf16[4,8,1024]{2,1,0:T(8,128)(2,1)}), bf16[4,1024,1024]{2,1,0:T(8,128)(2,1)}) %all-gather.5.cloned.1.call-update) | async-done | bytes 8388624 | tf_op jit(solution)/shard_map/all_gather | solution.py:101
  95.4 58.2 %while.10 = (s32[]{:T(128)}, bf16[2,1024,128]{2,1,0:T(8,128)(2,1)}, bf16[2,1024,4,32]{1,3,2,0:T(8,128)(2,1)}, s32[1024]{0:T(1024)S(1)}, bf16[2,1024,4,32]{1,3,2,...) while((s32[]{:T(128)}, bf16[2,1024,128]{2,1,0:T(8,128)(2,1)}, ...), condition=%wide.region_9.10_spmd, body=%wide.region_6.9_spmd.sunk | while | flops 885529600 | bytes 55126656 | solution.py:112
  95.4 8.6 %fusion.143 = f32[4,1024]{1,0:T(4,128)S(1)} fusion(bf16[4,1024,1024]{1,2,0:T(8,128)(2,1)} %get-tuple-element.237, pred[1024]{0:T(1024)(128)(4,1)S(1)} %broadcast_compare_fusion.3, bf16[2,1024,4,32]{1,3,2,0:T(8,128)(2,1)S(1)} %get-tuple-element.236, s32[]{:T(128)S(6)} %copy.142, bf16[2,1024,4,32]{1,3,2,0:T(8,128)(2,1)S(1)} %get-tuple-element.235), kind=kOutput, calls=%fused_computation.122.clone.1 | convolution fusion | flops 289408000 | bytes 8931328 | tf_op jit(solution)/shard_map/while/body/eval_jaxpr/sub | solution.py:41
  104.3 8.1 %fusion.144 = f32[4,1024,1024]{1,2,0:T(8,128)} fusion(bf16[2,1024,4,32]{1,3,2,0:T(8,128)(2,1)S(1)} %get-tuple-element.236, s32[]{:T(128)S(6)} %copy.142, bf16[2,1024,4,32]{1,3,2,0:T(8,128)(2,1)S(1)} %get-tuple-element.235), kind=kOutput, calls=%fused_computation.17.clone.1 | convolution fusion | flops 268435456 | bytes 17302528 | tf_op jit(solution)/shard_map/while/body/eval_jaxpr/qhd,khd->hqk/dot_general | solution.py:36
  112.4 10.8 %fusion.145 = bf16[1024,4,32]{0,2,1:T(8,128)(2,1)S(1)} fusion(f32[1024,4,32]{0,2,1:T(8,128)S(1)} %bitcast.153, f32[4,1024]{1,0:T(4,128)S(1)} %fusion.143, f32[4,1024,1024]{1,2,0:T(8,128)} %fusion.144, bf16[4,1024,1024]{1,2,0:T(8,128)(2,1)} %get-tuple-element.237, pred[1024]{0:T(1024)(128)(4,1)S(1)} %broadcast_compare_fusion.3, ...), kind=kOutput, calls=%fused_computation.12.clone.1 | convolution fusion | flops 293868544 | bytes 26231812 | tf_op jit(solution)/shard_map/while/body/eval_jaxpr/hqk,khd->qhd/dot_general | solution.py:43
  124.2 8.6 %fusion.143 = f32[4,1024]{1,0:T(4,128)S(1)} fusion(bf16[4,1024,1024]{1,2,0:T(8,128)(2,1)} %get-tuple-element.237, pred[1024]{0:T(1024)(128)(4,1)S(1)} %broadcast_compare_fusion.3, bf16[2,1024,4,32]{1,3,2,0:T(8,128)(2,1)S(1)} %get-tuple-element.236, s32[]{:T(128)S(6)} %copy.142, bf16[2,1024,4,32]{1,3,2,0:T(8,128)(2,1)S(1)} %get-tuple-element.235), kind=kOutput, calls=%fused_computation.122.clone.1 | convolution fusion | flops 289408000 | bytes 8931328 | tf_op jit(solution)/shard_map/while/body/eval_jaxpr/sub | solution.py:41
  133.0 8.1 %fusion.144 = f32[4,1024,1024]{1,2,0:T(8,128)} fusion(bf16[2,1024,4,32]{1,3,2,0:T(8,128)(2,1)S(1)} %get-tuple-element.236, s32[]{:T(128)S(6)} %copy.142, bf16[2,1024,4,32]{1,3,2,0:T(8,128)(2,1)S(1)} %get-tuple-element.235), kind=kOutput, calls=%fused_computation.17.clone.1 | convolution fusion | flops 268435456 | bytes 17302528 | tf_op jit(solution)/shard_map/while/body/eval_jaxpr/qhd,khd->hqk/dot_general | solution.py:36
  141.2 11.5 %fusion.145 = bf16[1024,4,32]{0,2,1:T(8,128)(2,1)S(1)} fusion(f32[1024,4,32]{0,2,1:T(8,128)S(1)} %bitcast.153, f32[4,1024]{1,0:T(4,128)S(1)} %fusion.143, f32[4,1024,1024]{1,2,0:T(8,128)} %fusion.144, bf16[4,1024,1024]{1,2,0:T(8,128)(2,1)} %get-tuple-element.237, pred[1024]{0:T(1024)(128)(4,1)S(1)} %broadcast_compare_fusion.3, ...), kind=kOutput, calls=%fused_computation.12.clone.1 | convolution fusion | flops 293868544 | bytes 26231812 | tf_op jit(solution)/shard_map/while/body/eval_jaxpr/hqk,khd->qhd/dot_general | solution.py:43
  153.6 13.2 %all-gather.3.cloned.1.call-done = bf16[4,1024,1024]{2,0,1:T(4,128)(2,1)} async-done(((bf16[4,8,1024]{2,0,1:T(4,128)(2,1)}), bf16[4,1024,1024]{2,0,1:T(4,128)(2,1)}) %all-gather.3.cloned.1.call-update) | async-done | bytes 8388624 | tf_op jit(solution)/shard_map/all_gather | solution.py:92
  166.8 12.1 %copy_convert_fusion = f32[4,1024,1024]{2,1,0:T(8,128)} fusion(bf16[4,1024,1024]{2,0,1:T(4,128)(2,1)} %all-gather.3.cloned.1.call-done), kind=kLoop, calls=%fused_computation.49 | loop fusion | flops 4194304 | bytes 25165824 | tf_op jit(solution)/shard_map/convert_element_type | solution.py:54
  178.8 16.5 %copy.88 = f32[4,1024,1024]{1,2,0:T(8,128)} copy(f32[4,1024,1024]{2,1,0:T(8,128)} %copy_convert_fusion) | data formatting | bytes 33554432 | tf_op jit(solution)/shard_map/convert_element_type | solution.py:54
  195.3 21.4 %fusion.110 = (f32[2,4,1024]{2,1,0:T(4,128)S(1)}, f32[2,4,1024,1024]{2,3,1,0:T(8,128)}) fusion(f32[4,1024,1024]{1,2,0:T(8,128)} %copy.88, pred[1024]{0:T(1024)(128)(4,1)S(1)} %copy-done.7, bf16[2,1024,4,32]{1,0,3,2:T(2,128)(2,1)S(1)} %copy-done.1, bf16[2,1024,4,32]{1,0,3,2:T(2,128)(2,1)S(1)} %copy-done.2), kind=kOutput, calls=%fused_computation.126 | convolution fusion | flops 570426368 | bytes 51414016 | tf_op jit(solution)/shard_map/sub | solution.py:58
  216.8 12.1 %fusion.56 = f32[2,1024,4,32]{1,3,2,0:T(8,128)S(1)} fusion(f32[2,4,1024,1024]{2,3,1,0:T(8,128)} %get-tuple-element.142, f32[2,4,1024]{2,1,0:T(4,128)S(1)} %get-tuple-element.141, bf16[2,1024,4,32]{1,0,3,2:T(2,128)(2,1)S(1)} %copy-done.3), kind=kOutput, calls=%fused_computation.64 | convolution fusion | flops 553648128 | bytes 35160064 | tf_op jit(solution)/shard_map/whqk,wkhd->wqhd/dot_general | solution.py:60
  230.3 2.4 %fusion.55 = bf16[2048,128]{1,0:T(8,128)(2,1)} fusion(f32[128]{0:T(128)S(1)} %copy-done.11, f32[2048,128]{1,0:T(8,128)S(1)} %copy.92, f32[2048,512]{1,0:T(8,128)} %copy-done, f32[128]{0:T(128)S(1)} %copy-done.10, bf16[2,128,128]{2,1,0:T(8,128)(2,1)S(1)} %get-tuple-element.246), kind=kOutput, calls=%fused_computation.63 | convolution fusion | flops 69206016 | bytes 2655232 | tf_op jit(solution)/shard_map/dot_general | solution.py:63
  (76 shorter events, 18.3 us)
Async XLA Ops:
  7.2 11.7 %copy-start.8 = (bf16[2,128,4]{1,2,0:T(4,128)(2,1)S(1)}, bf16[2,128,4]{1,2,0:T(4,128)(2,1)}, u32[]{:S(2)}) copy-start(bf16[2,128,4]{1,2,0:T(4,128)(2,1)} %param.16) | copy-start | bytes 6148
  7.2 88.2 %all-gather.5.cloned.1.call-start = ((), (), s32[]{:S(2)}) async-start(), calls=%async_computation.2 | async-start | bytes 8454144 | tf_op jit(solution)/shard_map/all_gather | solution.py:101
  9.4 26.6 %copy-start.5 = (bf16[2,128,512]{2,1,0:T(8,128)(2,1)S(1)}, bf16[2,128,512]{2,1,0:T(8,128)(2,1)}, u32[]{:S(2)}) copy-start(bf16[2,128,512]{2,1,0:T(8,128)(2,1)} %param.15) | copy-start | bytes 786436
  20.2 146.6 %all-gather.3.cloned.1.call-start = ((), (), s32[]{:S(2)}) async-start(), calls=%async_computation.1 | async-start | bytes 8454144 | tf_op jit(solution)/shard_map/all_gather | solution.py:92
  24.5 25.4 %all-to-all-start = ((bf16[8,128,2,128]{3,2,0,1:T(2,128)(2,1)}), bf16[8,128,2,128]{3,2,0,1:T(2,128)(2,1)S(1)}, u32[]{:S(2)}, u32[]{:S(2)}) async-start(bf16[8,128,2,128]{3,2,0,1:T(2,128)(2,1)} %copy.93), calls=%async_computation | async-start | bytes 1048576 | tf_op jit(solution)/shard_map/all_to_all | solution.py:99
  36.1 7.1 %copy-start.9 = (f32[2,128]{1,0:T(2,128)S(1)}, f32[2,128]{1,0:T(2,128)}, u32[]{:S(2)}) copy-start(f32[2,128]{1,0:T(2,128)} %param.17) | copy-start | bytes 3076
  36.1 7.1 %copy-start.12 = (f32[2,128]{1,0:T(2,128)S(1)}, f32[2,128]{1,0:T(2,128)}, u32[]{:S(2)}) copy-start(f32[2,128]{1,0:T(2,128)} %param.19) | copy-start | bytes 3076
  36.1 7.7 %copy-start.6 = (s32[1024]{0:T(1024)S(1)}, s32[1024]{0:T(1024)}, u32[]{:S(2)}) copy-start(s32[1024]{0:T(1024)} %param.12) | copy-start | bytes 12292
  36.8 2.0 copy-start
  54.4 41.0 %copy-start.4 = (bf16[2,128,128]{2,1,0:T(8,128)(2,1)S(1)}, bf16[2,128,128]{2,1,0:T(8,128)(2,1)}, u32[]{:S(2)}) copy-start(bf16[2,128,128]{2,1,0:T(8,128)(2,1)} %param.18) | copy-start | bytes 196612
  178.8 16.5 %copy-start.1 = (bf16[2,1024,4,32]{1,0,3,2:T(2,128)(2,1)S(1)}, bf16[2,1024,4,32]{1,0,3,2:T(2,128)(2,1)}, u32[]{:S(2)}) copy-start(bf16[2,1024,4,32]{1,0,3,2:T(2,128)(2,1)} %reshape.133) | copy-start | bytes 1572868
  178.8 16.5 %copy-start.2 = (bf16[2,1024,4,32]{1,0,3,2:T(2,128)(2,1)S(1)}, bf16[2,1024,4,32]{1,0,3,2:T(2,128)(2,1)}, u32[]{:S(2)}) copy-start(bf16[2,1024,4,32]{1,0,3,2:T(2,128)(2,1)} %reshape.132) | copy-start | bytes 1572868
  178.8 16.5 %copy-start.7 = (pred[1024]{0:T(1024)(128)(4,1)S(1)}, pred[1024]{0:T(1024)(128)(4,1)}, u32[]{:S(2)}) copy-start(pred[1024]{0:T(1024)(128)(4,1)} %broadcast_compare_fusion.1) | copy-start | bytes 3076
  195.3 21.4 %copy-start.3 = (bf16[2,1024,4,32]{1,0,3,2:T(2,128)(2,1)S(1)}, bf16[2,1024,4,32]{1,0,3,2:T(2,128)(2,1)}, u32[]{:S(2)}) copy-start(bf16[2,1024,4,32]{1,0,3,2:T(2,128)(2,1)} %reshape.131) | copy-start | bytes 1572868
  216.7 13.6 %copy-start.10 = (f32[128]{0:T(128)S(1)}, f32[128]{0:T(128)}, u32[]{:S(2)}) copy-start(f32[128]{0:T(128)} %get-tuple-element.134) | copy-start | bytes 1540
  216.7 13.6 %copy-start.11 = (f32[128]{0:T(128)S(1)}, f32[128]{0:T(128)}, u32[]{:S(2)}) copy-start(f32[128]{0:T(128)} %get-tuple-element.147) | copy-start | bytes 1540
Sparse Core Ops, SparseCore 0:
  20.3 75.0 all-gather.4
  98.4 68.3 all-gather.2
where the time goes:
time: 240 us
  matrix products  98.8 us (41%)
  waiting for transfers between devices  54.9 us (23%)
  local copies, waits for them, and re-layouts  32.8 us (14%)
  other arithmetic  27.1 us (11%)
  between operations  14.4 us (6%)
  starting transfers between devices  11.6 us (5%)
    all_gather x1, waiting for transfers between devices, body(): end_full = lax.all_gather(bias_end, ('row', 'col'), axis=1, tiled=True)  36.1 us
    dot_general x2, matrix products, attend(): jnp.einsum('hqk,khd->qhd', weights, value_rows, preferred_element_type=jn...  22.3 us
    sub x1, matrix products, attend_lines(): expo = jnp.exp(scores - top)  21.4 us
    sub x2, matrix products, attend(): expo = jnp.exp(scores - top)  17.2 us
    convert_element_type x1, local copies, waits for them, and re-layouts, attend_lines(): bias.astype(jnp.float32)[None]  16.5 us
    dot_general x2, matrix products, attend(): jnp.einsum('qhd,khd->hqk', queries, key_rows, preferred_element_type=jnp....  16.2 us
    all_gather x1, waiting for transfers between devices, body(): lax.all_gather(bias_start, ('row', 'col'), axis=1, tiled=True)  13.2 us
    dot_general x1, matrix products, attend_lines(): jnp.einsum('whqk,wkhd->wqhd', weights, value_rows, preferred_element_type...  12.1 us
  transfers between devices with their start and end apart: 3, of which 3 were waited for; matrix products, arithmetic and copies ran while one was open for 33% of the time, Pallas kernels for 0%

commit v1 on v0

v1 whole, which is shorter than its diff:
```python
import jax
import jax.numpy as jnp
from jax import lax
from jax.experimental import pallas as pl
from jax.experimental.pallas import tpu as pltpu
from jax.sharding import PartitionSpec as P

N, C, HEADS, DH, RD = 1024, 128, 4, 32, 8
BF, F32 = jnp.bfloat16, jnp.float32
MESH = pl.DeviceIdType.MESH
NT = (((1,), (1,)), ((), ()))
NEG = -1e30
EPS = 1e-05
ORDERS = ((2, 1, 0), (0, 2, 1), (1, 0, 2))
PICKED = (0, 1, 8, 9)


def tile_at(h, lt):
    if isinstance(h, int) and isinstance(lt, int):
        return (lt // 3 + h) % 3 * 12 + h * 3 + lt % 3
    return lax.rem(lt // 3 + h, 3) * 12 + h * 3 + lax.rem(lt, 3)


def device_of(z, x, y, core):
    return (z * 2 + x // 2, lax.rem(x, 2) * 8 + y * 2 + core)


def stats_norm(x):
    center = jnp.mean(x, -1, keepdims=True)
    d = x - center
    spread = jnp.mean(d * d, -1, keepdims=True)
    return d * lax.rsqrt(spread + EPS)


def norm(x, gain, shift):
    return (stats_norm(x) * gain + shift).astype(BF)


def body(
    pair, mask, gain, shift, w_proj, w_bias, gate_bias, w_out, out_bias,
    out0, out1,
    G, xf, pkf, pk, cols, rowsbuf, bacc, xb,
    wq, wo, gb, wkt, lnorm, qr, kp, kpt, vp, gate, acc, sA, sB, mA, mB, ost,
    ag_s, ag_r, aa_s, aa_r, ms_s, ms_r,
):
    row, col = lax.axis_index("row"), lax.axis_index("col")
    me = row * 16 + col
    z, x = row // 2, lax.rem(row, 2) * 2 + col // 8
    y, core = lax.rem(col // 2, 4), lax.rem(col, 2)
    pos = (z, x, y)
    partner = (row, col + 1 - 2 * core)
    barrier = pltpu.get_barrier_semaphore()

    def signal(dev):
        pl.semaphore_signal(barrier, inc=1, device_id=dev, device_id_type=MESH)

    def beside(axis, by):
        p = list(pos)
        p[axis] = lax.rem(p[axis] + by, 4)
        return device_of(*p, core)

    @pl.when(core == 0)
    def _():
        signal(partner)
        for axis in range(3):
            signal(beside(axis, 1))
            signal(beside(axis, 3))

    @pl.when(core == 1)
    def _():
        def one(d, _):
            @pl.when(d != me)
            def _():
                signal((d // 16, lax.rem(d, 16)))

            return 0

        lax.fori_loop(0, 128, one, 0)

    def pick(a, _):
        xf[...] = pair[a].astype(F32)
        for q in range(4):
            pkf[pl.ds(q * 8 + a, 64, stride=32), :] = xf[pl.ds(PICKED[q], 64, stride=16), :]
        return 0

    lax.fori_loop(0, RD, pick, 0)

    def pack(i, _):
        pk[pl.ds(i * 8, 8)] = pkf[pl.ds(pl.multiple_of(i * 256, 256), 256), :].reshape(8, 32, 128).astype(BF)
        return 0

    lax.fori_loop(0, 8, pack, 0)

    pl.semaphore_wait(barrier, 70 - 6 * core)

    def to_chip(c, _):
        @pl.when(2 * c + 1 != me)
        def _():
            pltpu.make_async_remote_copy(
                pk.at[c], cols.at[me], aa_s, aa_r, device_id=(c // 8, lax.rem(c, 8) * 2 + 1), device_id_type=MESH
            ).start()

        return 0

    lax.fori_loop(0, 64, to_chip, 0)

    rows_copy = pltpu.make_async_remote_copy(
        pair.at[pl.ds(0, 2)], rowsbuf, ms_s.at[0], ms_r.at[0], device_id=partner, device_id_type=MESH
    )

    @pl.when(core == 1)
    def _():
        rows_copy.start()
        cols[me] = pk[me // 2]

    wcat = []
    for p in range(2):
        w = jnp.concatenate([w_bias[p].astype(F32), jnp.zeros((128, 124), F32)], 1)
        wcat.append(jnp.transpose(w))
    zero8 = jnp.zeros((8, 128), F32)
    wrep = jnp.concatenate(
        [
            jnp.concatenate(
                [jnp.broadcast_to(wcat[p][h : h + 1], (8, 128)) if s == p else zero8 for s in range(2)], 1
            )
            for p in range(2)
            for h in range(4)
        ],
        0,
    )
    r8 = lax.rem(lax.broadcasted_iota(jnp.int32, (64, 256), 0), 8)

    def bias_row(a, _):
        lhs = jnp.where(r8 == a, wrep, 0.0).astype(BF)
        for b in range(4):
            xn = stats_norm(pair[a, b * 256 : (b + 1) * 256, :].astype(F32))
            both = jnp.concatenate([(xn * gain[p : p + 1] + shift[p : p + 1]).astype(BF) for p in range(2)], 1)
            part = lax.dot_general(lhs, both, NT, preferred_element_type=F32)
            s = slice(b * 256, (b + 1) * 256)
            bacc[:, s] = jnp.where(a == 0, 0.0, bacc[:, s]) + part
        return 0

    bacc[...] = jnp.zeros((64, N), F32)
    lax.fori_loop(0, RD, bias_row, 0)
    live = jnp.broadcast_to(mask[...], (8, N))
    lane8 = lax.broadcasted_iota(jnp.int32, (8, N), 1)
    sub8 = lax.broadcasted_iota(jnp.int32, (8, N), 0)
    own = jnp.sum(jnp.where(lane8 == me * 8 + sub8, live, 0), -1, keepdims=True)
    own = jnp.broadcast_to(own, (8, N))
    for ph in range(8):
        keep = (live if ph < 4 else own) > 0
        bacc[ph * 8 : ph * 8 + 8, :] = jnp.where(keep, bacc[ph * 8 : ph * 8 + 8, :], NEG)
    half_copy = pltpu.make_async_remote_copy(
        bacc.at[pl.ds(pl.multiple_of((1 - core) * 32, 32), 32)],
        xb, ms_s.at[1], ms_r.at[1], device_id=partner, device_id_type=MESH,
    )
    half_copy.start()

    def prep_weights():
        for q in range(4):
            for blk in range(4):
                w = w_proj[core, :, blk * 128 : (blk + 1) * 128].astype(F32)
                if q:
                    w = pltpu.roll(w, 32 * q, 1)
                wq[q, :, blk * 128 : (blk + 1) * 128] = w.astype(BF)
                if blk == 1:
                    wkt[q] = jnp.transpose(w).astype(BF)
            o = w_out[core].astype(F32)
            g = jnp.broadcast_to(gate_bias[pl.ds(core, 1)], (8, 128))
            if q:
                o = pltpu.roll(o, 32 * q, 0)
                g = pltpu.roll(g, 32 * q, 1)
            wo[q] = o.astype(BF)
            gb[q] = g
        vp[:, :, 128:] = jnp.ones((4, N, 128), BF)
        acc[...] = jnp.zeros_like(acc)

    prep_weights()

    half_copy.wait_recv()
    mine = pl.multiple_of(core * 32, 32)
    for h in range(4):
        ours = bacc[pl.ds(pl.multiple_of(mine + h * 8, 8), 8), :]
        theirs = xb[h * 8 : h * 8 + 8, :]
        low = jnp.where(core == 0, ours, theirs)
        high = jnp.where(core == 0, theirs, ours)
        block = jnp.concatenate([low, high], 0).astype(BF)
        for lt in range(8):
            G[z, x, y, tile_at(h, lt)] = block[:, lt * 128 : (lt + 1) * 128]
    for r in range(3):
        for h in range(4):
            if (r - h) % 3 == 2:
                G[z, x, y, r * 12 + h * 3 + 2] = jnp.zeros((16, 128), BF)

    def region(axis, at, free, tiles, half=None):
        index = list(pos)
        for f in free:
            index[f] = pl.ds(0, 4)
        if half is not None and free:
            index[free[0]] = pl.ds(2 * half, 2)
        if half is not None and not free:
            tiles = (tiles[0] + half * (tiles[1] // 2), tiles[1] // 2)
        index[axis] = at
        return G.at[index[0], index[1], index[2], pl.ds(tiles[0], tiles[1])]

    def ring(r, phase, h):
        axis, free = ORDERS[r][phase], ORDERS[r][:phase]
        if phase < 2:
            tiles, sem = (r * 12, 12), phase * 12 + r * 4
        else:
            tiles, sem = (r * 12 + h * 3, 2 if (r - h) % 3 == 2 else 3), 24 + h * 12 + r * 4
        v = pos[axis]
        up, down, far = lax.rem(v + 1, 4), lax.rem(v + 3, 4), lax.rem(v + 2, 4)

        def copy(at, half, k, to):
            ref = region(axis, at, free, tiles, half)
            return pltpu.make_async_remote_copy(
                ref, ref, ag_s.at[sem + k], ag_r.at[sem + k], device_id=beside(axis, to), device_id_type=MESH
            )

        sends = ((v, None, 0, 1), (v, None, 1, 3), (down, 0, 2, 1), (up, 1, 3, 3))
        gets = ((down, None, 0, 1), (up, None, 1, 3), (far, 0, 2, 1), (far, 1, 3, 3))
        return (lambda k: copy(*sends[k])), (lambda k: copy(*gets[k]))

    def start(phase, step, h=0):
        for r in range(3):
            sends, _ = ring(r, phase, h)
            for k in (2 * step, 2 * step + 1):
                sends(k).start()

    def arrive(phase, step, h=0):
        for r in range(3):
            _, gets = ring(r, phase, h)
            for k in (2 * step, 2 * step + 1):
                gets(k).wait_recv()

    def line(q):
        g, s = gain[pl.ds(core, 1)], shift[pl.ds(core, 1)]
        R = 256

        @pl.when(core == 0)
        def _():
            def step(i, _):
                rr = pl.ds(pl.multiple_of(i * R, R), R)
                src = pair[q, rr, :] if q < 2 else rowsbuf[q - 2, rr, :]
                lnorm[rr, :] = norm(src.astype(F32), g, s)
                return 0

            lax.fori_loop(0, N // R, step, 0)

        @pl.when(core == 1)
        def _():
            def step(i, _):
                rr = pl.ds(pl.multiple_of(i * R, R), R)
                v = cols[pl.ds(i * (R // 8), R // 8), q // 2 * 16 : q // 2 * 16 + 16, :].astype(F32)
                lnorm[rr, :] = norm(v[:, q % 2 * 8 : q % 2 * 8 + 8, :].reshape(R, 128), g, s)
                return 0

            lax.fori_loop(0, N // R, step, 0)

        def step(i, _):
            rr = pl.ds(pl.multiple_of(i * R, R), R)
            full = jnp.dot(lnorm[rr, :], wq[q], preferred_element_type=F32)
            qr[q, rr, :] = (full[:, :128] * DH**-0.5).astype(BF)
            k = full[:, 128:256].astype(BF)
            v = full[:, 256:384].astype(BF)
            for h in range(4):
                sl = slice(32 * ((q + h) % 4), 32 * ((q + h) % 4) + 32)
                kp[h, rr, sl] = k[:, sl]
                vp[h, rr, sl] = v[:, sl]
            gate[q, rr, :] = jax.nn.sigmoid(full[:, 384:] + gb[q, 0:1])
            return 0

        lax.fori_loop(0, N // R, step, 0)

        @pl.when(core == 0)
        def _():
            kt = lax.dot_general(wkt[q], lnorm[...], NT, preferred_element_type=F32).astype(BF)
            for h in range(4):
                s = (q + h) % 4
                kpt[h, 32 * s : 32 * s + 32, :] = kt[32 * s : 32 * s + 32, :]

    start(0, 0)

    @pl.when(core == 0)
    def _():
        rows_copy.wait_recv()

    @pl.when(core == 1)
    def _():
        rows_copy.wait_send()
        every = cols.at[pl.ds(0, 127)]
        pltpu.make_async_remote_copy(
            every, every, aa_s, aa_r, device_id=partner, device_id_type=MESH
        ).wait_recv()

    line(0)
    arrive(0, 0)
    start(0, 1)
    line(1)
    arrive(0, 1)
    start(1, 0)
    line(2)
    arrive(1, 0)
    start(1, 1)
    line(3)
    arrive(1, 1)
    start(2, 0, 0)
    start(2, 0, 1)
    arrive(2, 0, 0)
    start(2, 1, 0)
    start(2, 0, 2)
    arrive(2, 1, 0)

    lane = lax.broadcasted_iota(jnp.int32, (128, 128), 1)
    sub = lax.broadcasted_iota(jnp.int32, (128, 128), 0)
    slot = lane // 32

    def scores(c, h, jb, S, M):
        rows = pl.ds(pl.multiple_of(jb * 128, 128), 128)
        eye = (lane == sub).astype(F32).astype(BF)
        lhs = []
        for q in range(4):
            m = (slot == lax.rem(q + h, 4)).astype(F32).astype(BF)
            lhs.append(jnp.concatenate([qr[q, rows, :] * m, eye], 1))
        lhs = jnp.concatenate(lhs, 0)
        top = None
        for n in range(4):
            if c == 0:
                b = jnp.concatenate(
                    [
                        G[jb // 2, pl.ds(lax.rem(jb, 2) * 2, 2), :, tile_at(h, lt)].reshape(128, 128)
                        for lt in (2 * n, 2 * n + 1)
                    ],
                    1,
                )
                rhs = jnp.concatenate([kpt[h, :, n * 256 : (n + 1) * 256], b], 0)
                s = jnp.dot(lhs, rhs, preferred_element_type=F32)
            else:
                b = G[n, :, :, tile_at(h, jb)].reshape(256, 128)
                rhs = jnp.concatenate([kp[h, n * 256 : (n + 1) * 256, :], b], 1)
                s = lax.dot_general(lhs, rhs, NT, preferred_element_type=F32)
            S[:, n * 256 : (n + 1) * 256] = s
            t = jnp.maximum(s[:, :128], s[:, 128:])
            top = t if top is None else jnp.maximum(top, t)
        M[...] = jnp.broadcast_to(jnp.max(top, -1, keepdims=True), (512, 128))

    def mix(h, jb, S, M):
        rows = pl.ds(pl.multiple_of(jb * 128, 128), 128)
        p = jnp.exp(S[...] - jnp.concatenate([M[...]] * 8, 1)).astype(BF)
        o = jnp.dot(p, vp[h], preferred_element_type=F32)
        for q in range(4):
            oq = o[q * 128 : (q + 1) * 128]
            val = oq[:, :128] / oq[:, 128:] * gate[q, rows, :]
            acc[q, rows, :] = jnp.where(slot == lax.rem(q + h, 4), val, acc[q, rows, :])

    for c in range(2):
        pl.when(core == c)(lambda c=c: scores(c, 0, 0, sA, mA))

    def pair_of_units(i, _):
        @pl.when(i == 1)
        def _():
            arrive(2, 0, 1)
            start(2, 1, 1)
            start(2, 0, 3)

        @pl.when(i == 3)
        def _():
            arrive(2, 1, 1)

        @pl.when(i == 5)
        def _():
            arrive(2, 0, 2)
            start(2, 1, 2)

        @pl.when(i == 7)
        def _():
            arrive(2, 1, 2)

        @pl.when(i == 9)
        def _():
            arrive(2, 0, 3)
            start(2, 1, 3)

        @pl.when(i == 11)
        def _():
            arrive(2, 1, 3)

        u0 = 2 * i
        u1 = u0 + 1
        u2 = lax.rem(u0 + 2, 32)
        for c in range(2):

            @pl.when(core == c)
            def _(c=c):
                scores(c, u1 // 8, lax.rem(u1, 8), sB, mB)
                mix(u0 // 8, lax.rem(u0, 8), sA, mA)
                scores(c, u2 // 8, lax.rem(u2, 8), sA, mA)
                mix(u1 // 8, lax.rem(u1, 8), sB, mB)

        return 0

    lax.fori_loop(0, 16, pair_of_units, 0)

    def finish(jb, _):
        rows = pl.ds(pl.multiple_of(jb * 128, 128), 128)
        for q in range(4):
            o = jnp.dot(acc[q, rows, :].astype(BF), wo[q], preferred_element_type=F32)
            ost[q, rows, :] = (o + out_bias[pl.ds(core, 1)]).astype(BF)
        return 0

    lax.fori_loop(0, 8, finish, 0)

    for c, out in ((0, out0), (1, out1)):

        @pl.when(core == c)
        def _(c=c, out=out):
            away = pltpu.make_async_remote_copy(
                ost.at[pl.ds(2 - 2 * c, 2)], out, ms_s.at[2 + c], ms_r.at[2 + c], device_id=partner, device_id_type=MESH
            )
            away.start()
            home = pltpu.make_async_copy(ost.at[pl.ds(2 * c, 2)], out, ms_s.at[4])
            home.start()
            home.wait()
            away.wait_send()

    for c, out in ((1, out0), (0, out1)):

        @pl.when(core == c)
        def _(c=c, out=out):
            pltpu.make_async_remote_copy(
                ost.at[pl.ds(0, 2)], out, ms_s.at[3 - c], ms_r.at[3 - c], device_id=partner, device_id_type=MESH
            ).wait_recv()

    half_copy.wait_send()

    @pl.when(core == 0)
    def _():
        pltpu.make_async_remote_copy(pk, pk, aa_s, aa_r, device_id=partner, device_id_type=MESH).wait_send()

    @pl.when(core == 1)
    def _():
        most = pk.at[pl.ds(0, 63)]
        pltpu.make_async_remote_copy(most, most, aa_s, aa_r, device_id=partner, device_id_type=MESH).wait_send()

    for phase, heads in ((0, (0,)), (1, (0,)), (2, range(4))):
        for h in heads:
            for r in range(3):
                for k in range(4):
                    ring(r, phase, h)[0](k).wait_send()


def local(pair, residue_mask, ln_gain, ln_shift, w_proj, w_bias, gate_bias, w_out, out_bias):
    vmem = pl.BlockSpec(memory_space=pltpu.VMEM)
    out = jax.ShapeDtypeStruct((2, N, C), BF)
    V = pltpu.VMEM
    dma = pltpu.SemaphoreType.DMA
    return pl.pallas_call(
        body,
        out_shape=(out, out),
        in_specs=[vmem] * 9,
        out_specs=(pl.BlockSpec(memory_space=pl.ANY),) * 2,
        scratch_shapes=[
            V((4, 4, 4, 36, 16, 128), BF), V((N, C), F32), V((2048, C), F32), V((64, 32, C), BF), V((128, 32, C), BF),
            V((2, N, C), BF), V((64, N), F32), V((32, N), F32),
            V((4, 128, 512), BF), V((4, 128, 128), BF), V((4, 8, 128), F32), V((4, 128, 128), BF), V((N, C), BF),
            V((4, N, C), BF), V((4, N, C), BF), V((4, C, N), BF), V((4, N, 256), BF), V((4, N, C), F32), V((4, N, C), F32),
            V((512, N), F32), V((512, N), F32), V((512, 128), F32), V((512, 128), F32), V((4, N, C), BF),
            dma((72,)), dma((72,)), dma, dma, dma((5,)), dma((4,)),
        ],
        compiler_params=pltpu.CompilerParams(
            collective_id=0, has_side_effects=True, vmem_limit_bytes=56 * 2**20
        ),
        cost_estimate=pl.CostEstimate(flops=20 * 10**9, bytes_accessed=4 * 2**20, transcendentals=17 * 10**6),
    )(pair, residue_mask.reshape(1, N), ln_gain, ln_shift, w_proj, w_bias, gate_bias, w_out, out_bias)


def solution(mesh):
    return jax.shard_map(
        local,
        mesh=mesh,
        in_specs=(P(("row", "col"), None, None), P(), P(), P(), P(), P(), P(), P(), P()),
        out_specs=(P(("row", "col"), None, None), P(("row", "col"), None, None)),
        check_vma=False,
    )
```

time: 240 us -> 89.9 us (0.37)
  matrix products: 98.8 us -> 0 us
  Pallas kernels: 0 us -> 83.8 us
  waiting for transfers between devices: 54.9 us -> 0 us
  local copies, waits for them, and re-layouts: 32.8 us -> 5.17 us
  other arithmetic: 27.1 us -> 0 us
  between operations: 14.4 us -> 0.64 us
  starting transfers between devices: 11.6 us -> 0 us
    pallas_call x0 -> x1, Pallas kernels: none -> 83.8 us  [local(): pl.pallas_call(body, out_shape=(out, out), in_specs=[vmem] * 9, out_specs...]
    dot_general x12 -> x0, matrix products: 60.2 us -> none  [the longest x2 22.3 us: attend(): jnp.einsum('hqk,khd->qhd', weights, value_rows, preferred_element_type=jn...]
    all_gather x2 -> x0, waiting for transfers between devices: 49.3 us -> none  [the longest x1 36.1 us: body(): end_full = lax.all_gather(bias_end, ('row', 'col'), axis=1, tiled=True)]
    sub x3 -> x0, matrix products: 38.6 us -> none  [the longest x1 21.4 us: attend_lines(): expo = jnp.exp(scores - top)]
    convert_element_type x4 -> x0, other arithmetic: 17.9 us -> none  [the longest x1 12.1 us: attend_lines(): bias.astype(jnp.float32)[None]]
    convert_element_type x3 -> x0, local copies, waits for them, and re-layouts: 16.9 us -> none  [the longest x1 16.5 us: attend_lines(): bias.astype(jnp.float32)[None]]
    all_to_all x1 -> x0, starting transfers between devices: 11.5 us -> none  [body(): lax.all_to_all(picked, ('row', 'col'), split_axis=1, concat_axis=1, tiled...]
    reduce_sum x4 -> x0, other arithmetic: 6.81 us -> none  [the longest x2 4.26 us: layer_norm(): spread = jnp.mean(jnp.square(wide - center), -1, keepdims=True)]
  transfers between devices with their start and end apart: 3 -> 0, of which waited for: 3 -> 0; matrix products, arithmetic and copies ran while one was open for 33% -> 0% of each run, Pallas kernels for 0% -> 0%
where the time goes in v1:
time: 89.9 us; the launch traced here: 89.6 us
  Pallas kernels  83.8 us (93%)
  local copies, waits for them, and re-layouts  5.17 us (6%)
    pallas_call x1, Pallas kernels, local(): pl.pallas_call(body, out_shape=(out, out), in_specs=[vmem] * 9, out_specs...  83.8 us
    unnamed x3, local copies, waits for them, and re-layouts  5.17 us

profile of v1, /device:TPU:1, one launch (start us, length us, event | category | flops | bytes accessed | tf_op | source)
XLA Modules:
  0.0 89.6 jit_solution(9326576209580264949)
XLA Ops:
  0.6 1.4 %copy.11.w_bias = bf16[2,128,4]{2,1,0:T(8,128)(2,1)} copy(bf16[2,128,4]{1,2,0:T(4,128)(2,1)} %param.14) | data formatting | bytes 4096 | tf_op args[5]
  2.1 83.8 %shard_map.104 = (bf16[2,1024,128]{2,1,0:T(8,128)(2,1)}, bf16[2,1024,128]{2,1,0:T(8,128)(2,1)}) custom-call(bf16[8,1024,128]{2,1,0:T(8,128)(2,1)} %pair.1, s32[1,1024]{1,0:T(1,128)} %bitcast.1, f32[2,128]{1,0:T(2,128)} %gain.1, f32[2,128]{1,0:T(2,128)} %shift.1, bf16[2,128,512]{2,1,0:T(8,128)(2,1)} %w_proj.1, bf16[2,128,4]{2,1,0:T(8,128)(2,1)} %copy.11.w_bias, ...), custom_call_target="tpu_custom_call" | custom-call | flops 20000000000 | bytes 4194304 | tf_op jit(solution)/shard_map/pallas_call | solution.py:458
  85.9 1.9 %copy.14 = bf16[2,1024,128]{2,1,0:T(8,128)(2,1)} copy(bf16[2,1024,128]{2,1,0:T(8,128)(2,1)} %get-tuple-element.4) | data formatting | bytes 1048576
  87.8 1.9 %copy.15 = bf16[2,1024,128]{2,1,0:T(8,128)(2,1)} copy(bf16[2,1024,128]{2,1,0:T(8,128)(2,1)} %get-tuple-element.5) | data formatting | bytes 1048576

commit v2 on v1

--- a/solution.py
+++ b/solution.py
@@ -37,11 +37,11 @@
 
 
 def body(
-    pair, mask, gain, shift, w_proj, w_bias, gate_bias, w_out, out_bias,
+    pair_hbm, mask, gain, shift, w_proj, w_bias, gate_bias, w_out, out_bias,
     out0, out1,
-    G, xf, pkf, pk, cols, rowsbuf, bacc, xb,
+    G, pair, xf, pkf, pk, cols, rowsbuf, bacc, xb,
     wq, wo, gb, wkt, lnorm, qr, kp, kpt, vp, gate, acc, sA, sB, mA, mB, ost,
-    ag_s, ag_r, aa_s, aa_r, ms_s, ms_r,
+    ag_s, ag_r, aa_s, aa_r, ms_s, ms_r, ld_s,
 ):
     row, col = lax.axis_index("row"), lax.axis_index("col")
     me = row * 16 + col
@@ -59,31 +59,36 @@
         p[axis] = lax.rem(p[axis] + by, 4)
         return device_of(*p, core)
 
+    def load(a):
+        return pltpu.make_async_copy(pair_hbm.at[a], pair.at[a], ld_s.at[a])
+
+    for a in range(RD):
+        load(a).start()
+
     @pl.when(core == 0)
     def _():
         signal(partner)
         for axis in range(3):
-            signal(beside(axis, 1))
-            signal(beside(axis, 3))
+            for by in (1, 2, 3):
+                signal(beside(axis, by))
 
     @pl.when(core == 1)
     def _():
-        def one(d, _):
-            @pl.when(d != me)
-            def _():
-                signal((d // 16, lax.rem(d, 16)))
-
+        def one(i, _):
+            d = lax.rem(me + i, 128)
+            signal((d // 16, lax.rem(d, 16)))
             return 0
 
-        lax.fori_loop(0, 128, one, 0)
-
-    def pick(a, _):
+        lax.fori_loop(1, 128, one, 0)
+
+    def pick(a):
+        load(a).wait()
         xf[...] = pair[a].astype(F32)
         for q in range(4):
             pkf[pl.ds(q * 8 + a, 64, stride=32), :] = xf[pl.ds(PICKED[q], 64, stride=16), :]
-        return 0
-
-    lax.fori_loop(0, RD, pick, 0)
+
+    for a in range(RD):
+        pick(a)
 
     def pack(i, _):
         pk[pl.ds(i * 8, 8)] = pkf[pl.ds(pl.multiple_of(i * 256, 256), 256), :].reshape(8, 32, 128).astype(BF)
@@ -91,32 +96,41 @@
 
     lax.fori_loop(0, 8, pack, 0)
 
-    pl.semaphore_wait(barrier, 70 - 6 * core)
-
-    def to_chip(c, _):
-        @pl.when(2 * c + 1 != me)
-        def _():
-            pltpu.make_async_remote_copy(
-                pk.at[c], cols.at[me], aa_s, aa_r, device_id=(c // 8, lax.rem(c, 8) * 2 + 1), device_id_type=MESH
-            ).start()
-
-        return 0
-
-    lax.fori_loop(0, 64, to_chip, 0)
-
-    rows_copy = pltpu.make_async_remote_copy(
-        pair.at[pl.ds(0, 2)], rowsbuf, ms_s.at[0], ms_r.at[0], device_id=partner, device_id_type=MESH
-    )
-
-    @pl.when(core == 1)
-    def _():
-        rows_copy.start()
-        cols[me] = pk[me // 2]
+    def remote(src, dst, send, recv, dev):
+        return pltpu.make_async_remote_copy(src, dst, send, recv, device_id=dev, device_id_type=MESH)
+
+    def plus(v, k):
+        return lax.rem(v + k, 4)
+
+    def picked_send():
+        chip = me // 2
+
+        def one(i, _):
+            c = lax.rem(chip + i, 64)
+            remote(pk.at[c], cols.at[me], aa_s, aa_r, (c // 8, lax.rem(c, 8) * 2 + 1)).start()
+            return 0
+
+        lax.fori_loop(1, 64, one, 0)
+
+        @pl.when(core == 0)
+        def _():
+            remote(pk.at[chip], cols.at[me], aa_s, aa_r, partner).start()
+
+        @pl.when(core == 1)
+        def _():
+            cols[me] = pk[chip]
+
+    def picked_end():
+        @pl.when(core == 1)
+        def _():
+            every = cols.at[pl.ds(0, 127)]
+            remote(every, every, aa_s, aa_r, partner).wait_recv()
+
+    rows_copy = remote(pair.at[pl.ds(0, 2)], rowsbuf, ms_s.at[0], ms_r.at[0], partner)
 
     wcat = []
     for p in range(2):
-        w = jnp.concatenate([w_bias[p].astype(F32), jnp.zeros((128, 124), F32)], 1)
-        wcat.append(jnp.transpose(w))
+        wcat.append(w_bias[p].astype(F32))
     zero8 = jnp.zeros((8, 128), F32)
     wrep = jnp.concatenate(
         [
@@ -154,7 +168,12 @@
         bacc.at[pl.ds(pl.multiple_of((1 - core) * 32, 32), 32)],
         xb, ms_s.at[1], ms_r.at[1], device_id=partner, device_id_type=MESH,
     )
+    pl.semaphore_wait(barrier, 73 - 9 * core)
     half_copy.start()
+
+    @pl.when(core == 1)
+    def _():
+        rows_copy.start()
 
     def prep_weights():
         for q in range(4):
@@ -192,47 +211,59 @@
             if (r - h) % 3 == 2:
                 G[z, x, y, r * 12 + h * 3 + 2] = jnp.zeros((16, 128), BF)
 
-    def region(axis, at, free, tiles, half=None):
-        index = list(pos)
-        for f in free:
-            index[f] = pl.ds(0, 4)
-        if half is not None and free:
-            index[free[0]] = pl.ds(2 * half, 2)
-        if half is not None and not free:
-            tiles = (tiles[0] + half * (tiles[1] // 2), tiles[1] // 2)
-        index[axis] = at
-        return G.at[index[0], index[1], index[2], pl.ds(tiles[0], tiles[1])]
-
-    def ring(r, phase, h):
-        axis, free = ORDERS[r][phase], ORDERS[r][:phase]
-        if phase < 2:
-            tiles, sem = (r * 12, 12), phase * 12 + r * 4
-        else:
-            tiles, sem = (r * 12 + h * 3, 2 if (r - h) % 3 == 2 else 3), 24 + h * 12 + r * 4
-        v = pos[axis]
-        up, down, far = lax.rem(v + 1, 4), lax.rem(v + 3, 4), lax.rem(v + 2, 4)
-
-        def copy(at, half, k, to):
-            ref = region(axis, at, free, tiles, half)
-            return pltpu.make_async_remote_copy(
-                ref, ref, ag_s.at[sem + k], ag_r.at[sem + k], device_id=beside(axis, to), device_id_type=MESH
-            )
-
-        sends = ((v, None, 0, 1), (v, None, 1, 3), (down, 0, 2, 1), (up, 1, 3, 3))
-        gets = ((down, None, 0, 1), (up, None, 1, 3), (far, 0, 2, 1), (far, 1, 3, 3))
-        return (lambda k: copy(*sends[k])), (lambda k: copy(*gets[k]))
-
-    def start(phase, step, h=0):
+    names = {}
+
+    def sem(*name):
+        return names.setdefault(name, len(names))
+
+    def region(r, tiles, u, v, w):
+        index = [0, 0, 0]
+        for axis, at in zip(ORDERS[r], (u, v, w)):
+            index[axis] = at
+        return G.at[index[0], index[1], index[2], tiles]
+
+    def gather_copy(ref, name, axis, by):
+        return remote(ref, ref, ag_s.at[sem(*name)], ag_r.at[sem(*name)], beside(axis, by))
+
+    def jobs(kind, lo, n=1):
+        whole = pl.ds(0, 4)
         for r in range(3):
-            sends, _ = ring(r, phase, h)
-            for k in (2 * step, 2 * step + 1):
-                sends(k).start()
-
-    def arrive(phase, step, h=0):
-        for r in range(3):
-            _, gets = ring(r, phase, h)
-            for k in (2 * step, 2 * step + 1):
-                gets(k).wait_recv()
+            tiles = pl.ds(r * 12 + 3 * lo, 3 * n - ((r - lo - n + 1) % 3 == 2))
+            axes = ORDERS[r]
+            u, v, w = (pos[axis] for axis in axes)
+
+            def at(*where, r=r, tiles=tiles):
+                return region(r, tiles, *where)
+
+            own = [at(u, v, w)]
+            rest = [at(plus(u, j), v, w) for j in (1, 2, 3)]
+            lines = [at(whole, plus(v, j), w) for j in (1, 2, 3)]
+            if kind == "U":
+                for k in (1, 2, 3):
+                    yield (kind, r, lo, k), axes[0], k, (own,), at(plus(u, 4 - k), v, w)
+            if kind == "V":
+                for k in (1, 2, 3):
+                    yield (kind, r, lo, k), axes[1], k, (own, rest), at(whole, plus(v, 4 - k), w)
+            if kind in "AD":
+                for k in (1, 2, 3) if kind == "D" else (1, 3):
+                    yield (kind, r, lo, k), axes[2], k, (own, rest, lines), at(whole, whole, plus(w, 4 - k))
+            if kind == "B":
+                for k, half in ((1, pl.ds(0, 2)), (3, pl.ds(2, 2))):
+                    parts = ([at(half, whole, plus(w, 4 - k))],)
+                    yield (kind, r, lo, k), axes[2], k, parts, at(half, whole, plus(w, 2))
+
+    def start(step, *what):
+        for name, axis, k, parts, _ in jobs(*what):
+            for ref in parts[step]:
+                gather_copy(ref, name, axis, k).start()
+
+    def arrive(*what):
+        for name, axis, _, _, ref in jobs(*what):
+            gather_copy(ref, name, axis, 1).wait_recv()
+
+    def left(*what):
+        for name, axis, _, _, ref in jobs(*what):
+            gather_copy(ref, name, axis, 1).wait_send()
 
     def line(q):
         g, s = gain[pl.ds(core, 1)], shift[pl.ds(core, 1)]
@@ -280,37 +311,40 @@
                 s = (q + h) % 4
                 kpt[h, 32 * s : 32 * s + 32, :] = kt[32 * s : 32 * s + 32, :]
 
-    start(0, 0)
+    start(0, "U", 0)
+    start(0, "U", 1, 3)
+    start(0, "V", 0)
+    start(0, "D", 0)
+    picked_send()
+    for what in (("V", 1), ("D", 1), ("V", 2, 2), ("A", 2), ("A", 3)):
+        start(0, *what)
+    arrive("U", 0)
+    start(1, "V", 0)
+    start(1, "D", 0)
+    arrive("U", 1, 3)
+    start(1, "V", 1)
 
     @pl.when(core == 0)
     def _():
         rows_copy.wait_recv()
 
-    @pl.when(core == 1)
-    def _():
-        rows_copy.wait_send()
-        every = cols.at[pl.ds(0, 127)]
-        pltpu.make_async_remote_copy(
-            every, every, aa_s, aa_r, device_id=partner, device_id_type=MESH
-        ).wait_recv()
-
+    arrive("V", 0)
+    start(2, "D", 0)
+    start(1, "V", 2, 2)
+    start(1, "D", 1)
+    picked_end()
     line(0)
-    arrive(0, 0)
-    start(0, 1)
+    arrive("V", 1)
+    start(2, "D", 1)
     line(1)
-    arrive(0, 1)
-    start(1, 0)
+    start(1, "A", 2)
+    start(1, "A", 3)
+    arrive("V", 2, 2)
+    start(2, "A", 2)
+    start(2, "A", 3)
     line(2)
-    arrive(1, 0)
-    start(1, 1)
     line(3)
-    arrive(1, 1)
-    start(2, 0, 0)
-    start(2, 0, 1)
-    arrive(2, 0, 0)
-    start(2, 1, 0)
-    start(2, 0, 2)
-    arrive(2, 1, 0)
+    arrive("D", 0)
 
     lane = lax.broadcasted_iota(jnp.int32, (128, 128), 1)
     sub = lax.broadcasted_iota(jnp.int32, (128, 128), 0)
@@ -354,37 +388,41 @@
             val = oq[:, :128] / oq[:, 128:] * gate[q, rows, :]
             acc[q, rows, :] = jnp.where(slot == lax.rem(q + h, 4), val, acc[q, rows, :])
 
+    def finish(c, u0):
+        first = pl.multiple_of(lax.rem(u0, 8) * 128, 256)
+        rows = pl.ds(first, 256)
+        for q in range(4):
+            o = jnp.dot(acc[q, rows, :].astype(BF), wo[q], preferred_element_type=F32)
+            ost[q, rows, :] = (o + out_bias[c : c + 1]).astype(BF)
+        out = (out0, out1)[c].at[:, rows]
+        remote(ost.at[pl.ds(2 - 2 * c, 2), rows], out, ms_s.at[2 + c], ms_r.at[2 + c], partner).start()
+        pltpu.make_async_copy(ost.at[pl.ds(2 * c, 2), rows], out, ms_s.at[4]).start()
+
     for c in range(2):
         pl.when(core == c)(lambda c=c: scores(c, 0, 0, sA, mA))
 
     def pair_of_units(i, _):
-        @pl.when(i == 1)
-        def _():
-            arrive(2, 0, 1)
-            start(2, 1, 1)
-            start(2, 0, 3)
-
         @pl.when(i == 3)
         def _():
-            arrive(2, 1, 1)
-
-        @pl.when(i == 5)
-        def _():
-            arrive(2, 0, 2)
-            start(2, 1, 2)
+            arrive("D", 1)
+
+        @pl.when(i == 4)
+        def _():
+            arrive("A", 2)
+            start(0, "B", 2)
+
+        @pl.when(i == 6)
+        def _():
+            arrive("A", 3)
+            start(0, "B", 3)
 
         @pl.when(i == 7)
         def _():
-            arrive(2, 1, 2)
-
-        @pl.when(i == 9)
-        def _():
-            arrive(2, 0, 3)
-            start(2, 1, 3)
+            arrive("B", 2)
 
         @pl.when(i == 11)
         def _():
-            arrive(2, 1, 3)
+            arrive("B", 3)
 
         u0 = 2 * i
         u1 = u0 + 1
@@ -397,57 +435,49 @@
                 mix(u0 // 8, lax.rem(u0, 8), sA, mA)
                 scores(c, u2 // 8, lax.rem(u2, 8), sA, mA)
                 mix(u1 // 8, lax.rem(u1, 8), sB, mB)
+                pl.when(i >= 12)(lambda: finish(c, u0))
 
         return 0
 
     lax.fori_loop(0, 16, pair_of_units, 0)
-
-    def finish(jb, _):
-        rows = pl.ds(pl.multiple_of(jb * 128, 128), 128)
-        for q in range(4):
-            o = jnp.dot(acc[q, rows, :].astype(BF), wo[q], preferred_element_type=F32)
-            ost[q, rows, :] = (o + out_bias[pl.ds(core, 1)]).astype(BF)
-        return 0
-
-    lax.fori_loop(0, 8, finish, 0)
 
     for c, out in ((0, out0), (1, out1)):
 
         @pl.when(core == c)
         def _(c=c, out=out):
-            away = pltpu.make_async_remote_copy(
-                ost.at[pl.ds(2 - 2 * c, 2)], out, ms_s.at[2 + c], ms_r.at[2 + c], device_id=partner, device_id_type=MESH
-            )
-            away.start()
-            home = pltpu.make_async_copy(ost.at[pl.ds(2 * c, 2)], out, ms_s.at[4])
-            home.start()
-            home.wait()
-            away.wait_send()
+            pltpu.make_async_copy(ost.at[pl.ds(2 * c, 2)], out, ms_s.at[4]).wait()
+            remote(ost.at[pl.ds(2 - 2 * c, 2)], out, ms_s.at[2 + c], ms_r.at[2 + c], partner).wait_send()
 
     for c, out in ((1, out0), (0, out1)):
 
         @pl.when(core == c)
         def _(c=c, out=out):
-            pltpu.make_async_remote_copy(
-                ost.at[pl.ds(0, 2)], out, ms_s.at[3 - c], ms_r.at[3 - c], device_id=partner, device_id_type=MESH
-            ).wait_recv()
+            remote(ost.at[pl.ds(0, 2)], out, ms_s.at[3 - c], ms_r.at[3 - c], partner).wait_recv()
 
     half_copy.wait_send()
 
     @pl.when(core == 0)
     def _():
-        pltpu.make_async_remote_copy(pk, pk, aa_s, aa_r, device_id=partner, device_id_type=MESH).wait_send()
+        remote(pk, pk, aa_s, aa_r, partner).wait_send()
 
     @pl.when(core == 1)
     def _():
         most = pk.at[pl.ds(0, 63)]
-        pltpu.make_async_remote_copy(most, most, aa_s, aa_r, device_id=partner, device_id_type=MESH).wait_send()
-
-    for phase, heads in ((0, (0,)), (1, (0,)), (2, range(4))):
-        for h in heads:
-            for r in range(3):
-                for k in range(4):
-                    ring(r, phase, h)[0](k).wait_send()
+        remote(most, most, aa_s, aa_r, partner).wait_send()
+        rows_copy.wait_send()
+
+    for what in (
+        ("U", 0), ("U", 1, 3), ("V", 0), ("V", 1), ("V", 2, 2), ("D", 0), ("D", 1), ("A", 2), ("A", 3), ("B", 2), ("B", 3)
+    ):
+        left(*what)
+
+
+def hand_over(a, b, out0, out1, sems):
+    copies = [pltpu.make_async_copy(a, out0, sems.at[0]), pltpu.make_async_copy(b, out1, sems.at[1])]
+    for copy in copies:
+        copy.start()
+    for copy in copies:
+        copy.wait()
 
 
 def local(pair, residue_mask, ln_gain, ln_shift, w_proj, w_bias, gate_bias, w_out, out_bias):
@@ -455,24 +485,29 @@
     out = jax.ShapeDtypeStruct((2, N, C), BF)
     V = pltpu.VMEM
     dma = pltpu.SemaphoreType.DMA
-    return pl.pallas_call(
+    anywhere = pl.BlockSpec(memory_space=pl.ANY)
+    raw = pl.pallas_call(
         body,
         out_shape=(out, out),
-        in_specs=[vmem] * 9,
-        out_specs=(pl.BlockSpec(memory_space=pl.ANY),) * 2,
+        in_specs=[anywhere] + [vmem] * 8,
+        out_specs=(anywhere,) * 2,
         scratch_shapes=[
-            V((4, 4, 4, 36, 16, 128), BF), V((N, C), F32), V((2048, C), F32), V((64, 32, C), BF), V((128, 32, C), BF),
+            V((4, 4, 4, 36, 16, 128), BF), V((RD, N, C), BF), V((N, C), F32), V((2048, C), F32), V((64, 32, C), BF),
+            V((128, 32, C), BF),
             V((2, N, C), BF), V((64, N), F32), V((32, N), F32),
             V((4, 128, 512), BF), V((4, 128, 128), BF), V((4, 8, 128), F32), V((4, 128, 128), BF), V((N, C), BF),
             V((4, N, C), BF), V((4, N, C), BF), V((4, C, N), BF), V((4, N, 256), BF), V((4, N, C), F32), V((4, N, C), F32),
             V((512, N), F32), V((512, N), F32), V((512, 128), F32), V((512, 128), F32), V((4, N, C), BF),
-            dma((72,)), dma((72,)), dma, dma, dma((5,)), dma((4,)),
+            dma((120,)), dma((120,)), dma, dma, dma((5,)), dma((4,)), dma((8,)),
         ],
         compiler_params=pltpu.CompilerParams(
             collective_id=0, has_side_effects=True, vmem_limit_bytes=56 * 2**20
         ),
         cost_estimate=pl.CostEstimate(flops=20 * 10**9, bytes_accessed=4 * 2**20, transcendentals=17 * 10**6),
-    )(pair, residue_mask.reshape(1, N), ln_gain, ln_shift, w_proj, w_bias, gate_bias, w_out, out_bias)
+    )(pair, residue_mask.reshape(1, N), ln_gain, ln_shift, w_proj, jnp.transpose(w_bias, (0, 2, 1)), gate_bias, w_out, out_bias)
+    return pl.pallas_call(
+        hand_over, out_shape=(out, out), in_specs=[vmem] * 2, out_specs=(anywhere,) * 2, scratch_shapes=[dma((2,))]
+    )(*raw)
 
 
 def solution(mesh):

time: 89.9 us -> 80.6 us (0.90)
  local copies, waits for them, and re-layouts: 5.17 us -> 0 us
  Pallas kernels: 83.8 us -> 79.8 us
    unnamed x3 -> x0, local copies, waits for them, and re-layouts: 5.17 us -> none
    pallas_call x1 -> x2, Pallas kernels: 83.8 us -> 79.8 us  [the longest x1 77.6 us: local(): pl.pallas_call(body, out_shape=(out, out), in_specs=[anywhere] + [vmem] *...]
where the time goes in v2:
time: 80.6 us; the launch traced here: 80.5 us
  Pallas kernels  79.8 us (99%)
    pallas_call x1, Pallas kernels, local(): pl.pallas_call(body, out_shape=(out, out), in_specs=[anywhere] + [vmem] *...  77.6 us
    pallas_call x1, Pallas kernels, local(): pl.pallas_call(hand_over, out_shape=(out, out), in_specs=[vmem] * 2, out_...  2.18 us

profile of v2, /device:TPU:1, one launch (start us, length us, event | category | flops | bytes accessed | tf_op | source)
XLA Modules:
  0.0 80.5 jit_solution(578910556519824802)
XLA Ops:
  0.6 77.6 %shard_map.104 = (bf16[2,1024,128]{2,1,0:T(8,128)(2,1)}, bf16[2,1024,128]{2,1,0:T(8,128)(2,1)}) custom-call(bf16[8,1024,128]{2,1,0:T(8,128)(2,1)} %pair_hbm.1, s32[1,1024]{1,0:T(1,128)} %bitcast.2, f32[2,128]{1,0:T(2,128)} %gain.1, f32[2,128]{1,0:T(2,128)} %shift.1, bf16[2,128,512]{2,1,0:T(8,128)(2,1)} %w_proj.1, bf16[2,4,128]{2,1,0:T(4,128)(2,1)} %bitcast.3, ...), custom_call_target="tpu_custom_call" | custom-call | flops 20000000000 | bytes 4194304 | tf_op jit(solution)/shard_map/pallas_call | solution.py:489
  78.3 2.2 %shard_map.105 = (bf16[2,1024,128]{2,1,0:T(8,128)(2,1)}, bf16[2,1024,128]{2,1,0:T(8,128)(2,1)}) custom-call(bf16[2,1024,128]{2,1,0:T(8,128)(2,1)} %get-tuple-element.4.a, bf16[2,1024,128]{2,1,0:T(8,128)(2,1)} %get-tuple-element.5.b), custom_call_target="tpu_custom_call" | custom-call | tf_op jit(solution)/shard_map/pallas_call | solution.py:508

commit v3 on v2

--- a/solution.py
+++ b/solution.py
@@ -26,9 +26,12 @@
 
 
 def stats_norm(x):
-    center = jnp.mean(x, -1, keepdims=True)
-    d = x - center
-    spread = jnp.mean(d * d, -1, keepdims=True)
+    ones = jnp.ones((2 * C, C), BF)
+    d = x.astype(F32) - jnp.dot(x, ones[:C], preferred_element_type=F32) * (1 / C)
+    square = d * d
+    high = square.astype(BF)
+    low = (square - high.astype(F32)).astype(BF)
+    spread = jnp.dot(jnp.concatenate([high, low], 1), ones, preferred_element_type=F32) * (1 / C)
     return d * lax.rsqrt(spread + EPS)
 
 
@@ -40,7 +43,7 @@
     pair_hbm, mask, gain, shift, w_proj, w_bias, gate_bias, w_out, out_bias,
     out0, out1,
     G, pair, xf, pkf, pk, cols, rowsbuf, bacc, xb,
-    wq, wo, gb, wkt, lnorm, qr, kp, kpt, vp, gate, acc, sA, sB, mA, mB, ost,
+    wq, wo, gb, qr, kp, kpt, vp, gate, acc, sA, sB, mA, mB, ost,
     ag_s, ag_r, aa_s, aa_r, ms_s, ms_r, ld_s,
 ):
     row, col = lax.axis_index("row"), lax.axis_index("col")
@@ -146,12 +149,9 @@
 
     def bias_row(a, _):
         lhs = jnp.where(r8 == a, wrep, 0.0).astype(BF)
-        for b in range(4):
-            xn = stats_norm(pair[a, b * 256 : (b + 1) * 256, :].astype(F32))
-            both = jnp.concatenate([(xn * gain[p : p + 1] + shift[p : p + 1]).astype(BF) for p in range(2)], 1)
-            part = lax.dot_general(lhs, both, NT, preferred_element_type=F32)
-            s = slice(b * 256, (b + 1) * 256)
-            bacc[:, s] = jnp.where(a == 0, 0.0, bacc[:, s]) + part
+        xn = stats_norm(pair[a])
+        both = jnp.concatenate([(xn * gain[p : p + 1] + shift[p : p + 1]).astype(BF) for p in range(2)], 1)
+        bacc[...] += lax.dot_general(lhs, both, NT, preferred_element_type=F32)
         return 0
 
     bacc[...] = jnp.zeros((64, N), F32)
@@ -182,8 +182,6 @@
                 if q:
                     w = pltpu.roll(w, 32 * q, 1)
                 wq[q, :, blk * 128 : (blk + 1) * 128] = w.astype(BF)
-                if blk == 1:
-                    wkt[q] = jnp.transpose(w).astype(BF)
             o = w_out[core].astype(F32)
             g = jnp.broadcast_to(gate_bias[pl.ds(core, 1)], (8, 128))
             if q:
@@ -261,96 +259,84 @@
         for name, axis, _, _, ref in jobs(*what):
             gather_copy(ref, name, axis, 1).wait_recv()
 
+    def start_all(*what):
+        for name, axis, k, parts, _ in jobs(*what):
+            for step in parts:
+                for ref in step:
+                    gather_copy(ref, name, axis, k).start()
+
     def left(*what):
         for name, axis, _, _, ref in jobs(*what):
             gather_copy(ref, name, axis, 1).wait_send()
 
     def line(q):
         g, s = gain[pl.ds(core, 1)], shift[pl.ds(core, 1)]
-        R = 256
-
-        @pl.when(core == 0)
-        def _():
-            def step(i, _):
-                rr = pl.ds(pl.multiple_of(i * R, R), R)
-                src = pair[q, rr, :] if q < 2 else rowsbuf[q - 2, rr, :]
-                lnorm[rr, :] = norm(src.astype(F32), g, s)
-                return 0
-
-            lax.fori_loop(0, N // R, step, 0)
-
-        @pl.when(core == 1)
-        def _():
-            def step(i, _):
-                rr = pl.ds(pl.multiple_of(i * R, R), R)
-                v = cols[pl.ds(i * (R // 8), R // 8), q // 2 * 16 : q // 2 * 16 + 16, :].astype(F32)
-                lnorm[rr, :] = norm(v[:, q % 2 * 8 : q % 2 * 8 + 8, :].reshape(R, 128), g, s)
-                return 0
-
-            lax.fori_loop(0, N // R, step, 0)
-
-        def step(i, _):
-            rr = pl.ds(pl.multiple_of(i * R, R), R)
-            full = jnp.dot(lnorm[rr, :], wq[q], preferred_element_type=F32)
-            qr[q, rr, :] = (full[:, :128] * DH**-0.5).astype(BF)
-            k = full[:, 128:256].astype(BF)
+
+        def project(rows):
+            full = jnp.dot(norm(rows, g, s), wq[q], preferred_element_type=F32)
+            qr[q] = (full[:, :128] * DH**-0.5).astype(BF)
             v = full[:, 256:384].astype(BF)
             for h in range(4):
                 sl = slice(32 * ((q + h) % 4), 32 * ((q + h) % 4) + 32)
-                kp[h, rr, sl] = k[:, sl]
-                vp[h, rr, sl] = v[:, sl]
-            gate[q, rr, :] = jax.nn.sigmoid(full[:, 384:] + gb[q, 0:1])
-            return 0
-
-        lax.fori_loop(0, N // R, step, 0)
+                vp[h, :, sl] = v[:, sl]
+            gate[q] = jax.nn.sigmoid(full[:, 384:] + gb[q, 0:1])
+            return full[:, 128:256].astype(BF)
 
         @pl.when(core == 0)
         def _():
-            kt = lax.dot_general(wkt[q], lnorm[...], NT, preferred_element_type=F32).astype(BF)
+            kt = jnp.transpose(project(pair[q] if q < 2 else rowsbuf[q - 2]))
             for h in range(4):
-                s = (q + h) % 4
-                kpt[h, 32 * s : 32 * s + 32, :] = kt[32 * s : 32 * s + 32, :]
+                sl = slice(32 * ((q + h) % 4), 32 * ((q + h) % 4) + 32)
+                kpt[h, sl, :] = kt[sl]
+
+        @pl.when(core == 1)
+        def _():
+            rows = cols[:, q // 2 * 16 : q // 2 * 16 + 16, :].astype(F32)
+            k = project(rows[:, q % 2 * 8 : q % 2 * 8 + 8, :].reshape(N, C).astype(BF))
+            for h in range(4):
+                sl = slice(32 * ((q + h) % 4), 32 * ((q + h) % 4) + 32)
+                kp[h, :, sl] = k[:, sl]
+
+    def rows_ready():
+        @pl.when(core == 0)
+        def _():
+            rows_copy.wait_recv()
 
     start(0, "U", 0)
     start(0, "U", 1, 3)
-    start(0, "V", 0)
-    start(0, "D", 0)
     picked_send()
-    for what in (("V", 1), ("D", 1), ("V", 2, 2), ("A", 2), ("A", 3)):
-        start(0, *what)
     arrive("U", 0)
-    start(1, "V", 0)
-    start(1, "D", 0)
+    start_all("V", 0)
     arrive("U", 1, 3)
-    start(1, "V", 1)
-
-    @pl.when(core == 0)
-    def _():
-        rows_copy.wait_recv()
-
+    start_all("V", 1, 3)
+    rows_ready()
     arrive("V", 0)
-    start(2, "D", 0)
-    start(1, "V", 2, 2)
-    start(1, "D", 1)
+    start_all("A", 0)
+    arrive("V", 1, 3)
+    start_all("A", 1)
     picked_end()
     line(0)
-    arrive("V", 1)
-    start(2, "D", 1)
     line(1)
-    start(1, "A", 2)
-    start(1, "A", 3)
-    arrive("V", 2, 2)
-    start(2, "A", 2)
-    start(2, "A", 3)
     line(2)
     line(3)
-    arrive("D", 0)
+    arrive("A", 0)
+    start(0, "B", 0)
+    start_all("A", 2)
+    arrive("A", 1)
+    start(0, "B", 1)
+    arrive("B", 0)
 
     lane = lax.broadcasted_iota(jnp.int32, (128, 128), 1)
     sub = lax.broadcasted_iota(jnp.int32, (128, 128), 0)
     slot = lane // 32
-
-    def scores(c, h, jb, S, M):
+    slot2 = lax.broadcasted_iota(jnp.int32, (256, 128), 1) // 32
+
+    def scores(c, p, S, M):
+        for part in range(2):
+            half = pl.ds(512 * part, 512)
+            scores_of(c, p // 4, lax.rem(p, 4) * 2 + part, S.at[half], M.at[half])
+
+    def scores_of(c, h, jb, S, M):
         rows = pl.ds(pl.multiple_of(jb * 128, 128), 128)
         eye = (lane == sub).astype(F32).astype(BF)
         lhs = []
@@ -379,18 +365,17 @@
             top = t if top is None else jnp.maximum(top, t)
         M[...] = jnp.broadcast_to(jnp.max(top, -1, keepdims=True), (512, 128))
 
-    def mix(h, jb, S, M):
-        rows = pl.ds(pl.multiple_of(jb * 128, 128), 128)
-        p = jnp.exp(S[...] - jnp.concatenate([M[...]] * 8, 1)).astype(BF)
-        o = jnp.dot(p, vp[h], preferred_element_type=F32)
+    def mix(p, S, M):
+        h, rows = p // 4, pl.ds(pl.multiple_of(lax.rem(p, 4) * 256, 256), 256)
+        weights = jnp.exp(S[...] - jnp.concatenate([M[...]] * 8, 1)).astype(BF)
+        o = jnp.dot(weights, vp[h], preferred_element_type=F32)
         for q in range(4):
-            oq = o[q * 128 : (q + 1) * 128]
+            oq = jnp.concatenate([o[q * 128 : (q + 1) * 128], o[512 + q * 128 : 640 + q * 128]], 0)
             val = oq[:, :128] / oq[:, 128:] * gate[q, rows, :]
-            acc[q, rows, :] = jnp.where(slot == lax.rem(q + h, 4), val, acc[q, rows, :])
-
-    def finish(c, u0):
-        first = pl.multiple_of(lax.rem(u0, 8) * 128, 256)
-        rows = pl.ds(first, 256)
+            acc[q, rows, :] = jnp.where(slot2 == lax.rem(q + h, 4), val, acc[q, rows, :])
+
+    def finish(c, p):
+        rows = pl.ds(pl.multiple_of(lax.rem(p, 4) * 256, 256), 256)
         for q in range(4):
             o = jnp.dot(acc[q, rows, :].astype(BF), wo[q], preferred_element_type=F32)
             ost[q, rows, :] = (o + out_bias[c : c + 1]).astype(BF)
@@ -399,47 +384,48 @@
         pltpu.make_async_copy(ost.at[pl.ds(2 * c, 2), rows], out, ms_s.at[4]).start()
 
     for c in range(2):
-        pl.when(core == c)(lambda c=c: scores(c, 0, 0, sA, mA))
-
-    def pair_of_units(i, _):
-        @pl.when(i == 3)
-        def _():
-            arrive("D", 1)
-
-        @pl.when(i == 4)
-        def _():
-            arrive("A", 2)
-            start(0, "B", 2)
-
-        @pl.when(i == 6)
-        def _():
-            arrive("A", 3)
-            start(0, "B", 3)
-
-        @pl.when(i == 7)
-        def _():
-            arrive("B", 2)
-
-        @pl.when(i == 11)
-        def _():
-            arrive("B", 3)
-
-        u0 = 2 * i
-        u1 = u0 + 1
-        u2 = lax.rem(u0 + 2, 32)
-        for c in range(2):
-
-            @pl.when(core == c)
-            def _(c=c):
-                scores(c, u1 // 8, lax.rem(u1, 8), sB, mB)
-                mix(u0 // 8, lax.rem(u0, 8), sA, mA)
-                scores(c, u2 // 8, lax.rem(u2, 8), sA, mA)
-                mix(u1 // 8, lax.rem(u1, 8), sB, mB)
-                pl.when(i >= 12)(lambda: finish(c, u0))
+        pl.when(core == c)(lambda c=c: scores(c, 0, sA, mA))
+
+    def event0():
+        start_all("A", 3)
+
+    def event2():
+        arrive("A", 2)
+        start(0, "B", 2)
+
+    def event3():
+        arrive("B", 1)
+
+    def event6():
+        arrive("A", 3)
+        start(0, "B", 3)
+
+    def event7():
+        arrive("B", 2)
+
+    def event11():
+        arrive("B", 3)
+
+    events = {0: event0, 2: event2, 3: event3, 6: event6, 7: event7, 11: event11}
+
+    def pairs(i, _):
+        for odd in range(2):
+            p = 2 * i + odd
+            for when, event in events.items():
+                if when % 2 == odd:
+                    pl.when(i == when // 2)(event)
+            now, later = ((sA, mA), (sB, mB))[:: 1 - 2 * odd]
+            for c in range(2):
+
+                @pl.when(core == c)
+                def _(c=c, p=p, now=now, later=later):
+                    scores(c, lax.rem(p + 1, 16), *later)
+                    mix(p, *now)
+                    pl.when(i >= 6)(lambda: finish(c, p))
 
         return 0
 
-    lax.fori_loop(0, 16, pair_of_units, 0)
+    lax.fori_loop(0, 8, pairs, 0)
 
     for c, out in ((0, out0), (1, out1)):
 
@@ -467,7 +453,7 @@
         rows_copy.wait_send()
 
     for what in (
-        ("U", 0), ("U", 1, 3), ("V", 0), ("V", 1), ("V", 2, 2), ("D", 0), ("D", 1), ("A", 2), ("A", 3), ("B", 2), ("B", 3)
+        ("U", 0), ("U", 1, 3), ("V", 0), ("V", 1, 3), ("A", 0), ("A", 1), ("B", 0), ("A", 2), ("B", 1), ("A", 3), ("B", 2), ("B", 3)
     ):
         left(*what)
 
@@ -495,9 +481,9 @@
             V((4, 4, 4, 36, 16, 128), BF), V((RD, N, C), BF), V((N, C), F32), V((2048, C), F32), V((64, 32, C), BF),
             V((128, 32, C), BF),
             V((2, N, C), BF), V((64, N), F32), V((32, N), F32),
-            V((4, 128, 512), BF), V((4, 128, 128), BF), V((4, 8, 128), F32), V((4, 128, 128), BF), V((N, C), BF),
+            V((4, 128, 512), BF), V((4, 128, 128), BF), V((4, 8, 128), F32),
             V((4, N, C), BF), V((4, N, C), BF), V((4, C, N), BF), V((4, N, 256), BF), V((4, N, C), F32), V((4, N, C), F32),
-            V((512, N), F32), V((512, N), F32), V((512, 128), F32), V((512, 128), F32), V((4, N, C), BF),
+            V((1024, N), F32), V((1024, N), F32), V((1024, 128), F32), V((1024, 128), F32), V((4, N, C), BF),
             dma((120,)), dma((120,)), dma, dma, dma((5,)), dma((4,)), dma((8,)),
         ],
         compiler_params=pltpu.CompilerParams(

time: 80.6 us -> 76 us (0.943)
  Pallas kernels: 79.8 us -> 75.1 us
    pallas_call x1, Pallas kernels: 77.6 us -> 72.9 us  [local(): pl.pallas_call(body, out_shape=(out, out), in_specs=[anywhere] + [vmem] *...]
where the time goes in v3:
time: 76 us; the launch traced here: 75.9 us
  Pallas kernels  75.1 us (99%)
  between operations  0.8 us (1%)
    pallas_call x1, Pallas kernels, local(): pl.pallas_call(body, out_shape=(out, out), in_specs=[anywhere] + [vmem] *...  72.9 us
    pallas_call x1, Pallas kernels, local(): pl.pallas_call(hand_over, out_shape=(out, out), in_specs=[vmem] * 2, out_...  2.18 us

profile of v3, /device:TPU:1, one launch (start us, length us, event | category | flops | bytes accessed | tf_op | source)
XLA Modules:
  0.0 75.9 jit_solution(16561839287577438144)
XLA Ops:
  0.6 72.9 %shard_map.104 = (bf16[2,1024,128]{2,1,0:T(8,128)(2,1)}, bf16[2,1024,128]{2,1,0:T(8,128)(2,1)}) custom-call(bf16[8,1024,128]{2,1,0:T(8,128)(2,1)} %pair_hbm.1, s32[1,1024]{1,0:T(1,128)} %bitcast.2, f32[2,128]{1,0:T(2,128)} %gain.1, f32[2,128]{1,0:T(2,128)} %shift.1, bf16[2,128,512]{2,1,0:T(8,128)(2,1)} %w_proj.1, bf16[2,4,128]{2,1,0:T(4,128)(2,1)} %bitcast.3, ...), custom_call_target="tpu_custom_call" | custom-call | flops 20000000000 | bytes 4194304 | tf_op jit(solution)/shard_map/pallas_call | solution.py:475
  73.5 2.2 %shard_map.105 = (bf16[2,1024,128]{2,1,0:T(8,128)(2,1)}, bf16[2,1024,128]{2,1,0:T(8,128)(2,1)}) custom-call(bf16[2,1024,128]{2,1,0:T(8,128)(2,1)} %get-tuple-element.4.a, bf16[2,1024,128]{2,1,0:T(8,128)(2,1)} %get-tuple-element.5.b), custom_call_target="tpu_custom_call" | custom-call | tf_op jit(solution)/shard_map/pallas_call | solution.py:494

commit v4 on v3

--- a/solution.py
+++ b/solution.py
@@ -168,13 +168,6 @@
         bacc.at[pl.ds(pl.multiple_of((1 - core) * 32, 32), 32)],
         xb, ms_s.at[1], ms_r.at[1], device_id=partner, device_id_type=MESH,
     )
-    pl.semaphore_wait(barrier, 73 - 9 * core)
-    half_copy.start()
-
-    @pl.when(core == 1)
-    def _():
-        rows_copy.start()
-
     def prep_weights():
         for q in range(4):
             for blk in range(4):
@@ -193,6 +186,12 @@
         acc[...] = jnp.zeros_like(acc)
 
     prep_weights()
+    pl.semaphore_wait(barrier, 73 - 9 * core)
+    half_copy.start()
+
+    @pl.when(core == 1)
+    def _():
+        rows_copy.start()
 
     half_copy.wait_recv()
     mine = pl.multiple_of(core * 32, 32)
@@ -458,12 +457,17 @@
         left(*what)
 
 
-def hand_over(a, b, out0, out1, sems):
-    copies = [pltpu.make_async_copy(a, out0, sems.at[0]), pltpu.make_async_copy(b, out1, sems.at[1])]
-    for copy in copies:
-        copy.start()
-    for copy in copies:
-        copy.wait()
+def hand_over(a, b, out0, out1, held, sems):
+    parts = [(i, src.at[w], held.at[2 * i + w], dst.at[w]) for i, (src, dst) in enumerate(((a, out0), (b, out1))) for w in range(2)]
+    reads = [pltpu.make_async_copy(src, mid, sems.at[0, n]) for n, (_, src, mid, _) in enumerate(parts)]
+    writes = [pltpu.make_async_copy(mid, dst, sems.at[1, n]) for n, (_, _, mid, dst) in enumerate(parts)]
+    for read in reads:
+        read.start()
+    for read, write in zip(reads, writes):
+        read.wait()
+        write.start()
+    for write in writes:
+        write.wait()
 
 
 def local(pair, residue_mask, ln_gain, ln_shift, w_proj, w_bias, gate_bias, w_out, out_bias):
@@ -492,7 +496,8 @@
         cost_estimate=pl.CostEstimate(flops=20 * 10**9, bytes_accessed=4 * 2**20, transcendentals=17 * 10**6),
     )(pair, residue_mask.reshape(1, N), ln_gain, ln_shift, w_proj, jnp.transpose(w_bias, (0, 2, 1)), gate_bias, w_out, out_bias)
     return pl.pallas_call(
-        hand_over, out_shape=(out, out), in_specs=[vmem] * 2, out_specs=(anywhere,) * 2, scratch_shapes=[dma((2,))]
+        hand_over, out_shape=(out, out), in_specs=[anywhere] * 2, out_specs=(anywhere,) * 2,
+        scratch_shapes=[V((4, N, C), BF), dma((2, 4))],
     )(*raw)
 
 

time: 76 us -> 76.7 us (level)
    pallas_call x1, Pallas kernels: 72.9 us -> 73.7 us  [local(): pl.pallas_call(body, out_shape=(out, out), in_specs=[anywhere] + [vmem] *...]
where the time goes in v4:
time: 76.7 us; the launch traced here: 76.5 us
  Pallas kernels  75.7 us (99%)
  between operations  0.8 us (1%)
    pallas_call x1, Pallas kernels, local(): pl.pallas_call(body, out_shape=(out, out), in_specs=[anywhere] + [vmem] *...  73.7 us
    pallas_call x1, Pallas kernels, local(): pl.pallas_call(hand_over, out_shape=(out, out), in_specs=[anywhere] * 2,...  1.98 us

profile of v4, /device:TPU:1, one launch (start us, length us, event | category | flops | bytes accessed | tf_op | source)
XLA Modules:
  0.0 76.5 jit_solution(11696431303262582869)
XLA Ops:
  0.6 73.7 %shard_map.104 = (bf16[2,1024,128]{2,1,0:T(8,128)(2,1)}, bf16[2,1024,128]{2,1,0:T(8,128)(2,1)}) custom-call(bf16[8,1024,128]{2,1,0:T(8,128)(2,1)} %pair_hbm.1, s32[1,1024]{1,0:T(1,128)} %bitcast.2, f32[2,128]{1,0:T(2,128)} %gain.1, f32[2,128]{1,0:T(2,128)} %shift.1, bf16[2,128,512]{2,1,0:T(8,128)(2,1)} %w_proj.1, bf16[2,4,128]{2,1,0:T(4,128)(2,1)} %bitcast.3, ...), custom_call_target="tpu_custom_call" | custom-call | flops 20000000000 | bytes 4194304 | tf_op jit(solution)/shard_map/pallas_call | solution.py:479
  74.4 2.0 %shard_map.105 = (bf16[2,1024,128]{2,1,0:T(8,128)(2,1)}, bf16[2,1024,128]{2,1,0:T(8,128)(2,1)}) custom-call(bf16[2,1024,128]{2,1,0:T(8,128)(2,1)} %get-tuple-element.4.a, bf16[2,1024,128]{2,1,0:T(8,128)(2,1)} %get-tuple-element.5.b), custom_call_target="tpu_custom_call" | custom-call | tf_op jit(solution)/shard_map/pallas_call | solution.py:498
